TPU v7x, 128 devices: a whole 4x4x4 slice. The times are simulated.
128 devices in a mesh: lat: 4 (over z), lon: 32 (over x, y, core).
Axes of the slice: x: 4, y: 4, z: 4, core: 2. Of those that a mesh axis runs over, the one named last changes fastest.
Arguments:
- fields: bfloat16 [4, 69, 96, 4096], P(None, None, 'lat', 'lon'), may hold values from -6 to 6
- conv_weight: bfloat16 [9, 128, 69], replicated, may hold values from -0.25 to 0.25
- kv_weight: bfloat16 [512, 128], replicated, may hold values from -0.5 to 0.5
- out_weight: bfloat16 [256, 256], replicated, may hold values from -0.375 to 0.375
- norm_gain: float32 [256], replicated, may hold values from 0.5 to 1.5
- queries: bfloat16 [256, 256], replicated, may hold values from -64 to 64
Outputs:
- features: bfloat16 [4, 128, 96, 4096], P(None, None, 'lat', 'lon')
- latents: float32 [4, 256, 256], replicated
All inputs are finite; a program needn't handle non-finite values.
Results may differ from a plain program's by a relative error of at most 0.0035.
The roundings to bfloat16 on the way count: a program that leaves them out, or rounds other values in their place, can miss the bound.
Values may be sent and summed in bfloat16 or wider, within the bound.
A program may use at most 320 MiB of HBM per device.

v0:
```python
import jax
import jax.numpy as jnp
from jax import lax
from jax.sharding import PartitionSpec as P

DL = 256
Q = 256
HEADS = 4
HD = 64
BLK = 8


def extended(block, sides, width, periodic):
    for axis, dim in sides:
        count = lax.axis_size(axis)
        forward = [(i, i + 1) for i in range(count - 1)]
        if periodic:
            forward.append((count - 1, 0))
        backward = [(target, source) for source, target in forward]
        low = lax.ppermute(
            lax.slice_in_dim(block, block.shape[dim] - width, None, axis=dim), axis, forward
        )
        high = lax.ppermute(lax.slice_in_dim(block, 0, width, axis=dim), axis, backward)
        block = jnp.concatenate([low, block, high], axis=dim)
    return block


def convolve_block(window_in, conv_weight, lat_rows, lon_cols):
    running = jnp.zeros((window_in.shape[0], conv_weight.shape[1], lat_rows, lon_cols), jnp.float32)
    for tap_index in range(9):
        row_off = tap_index // 3
        col_off = tap_index % 3
        piece = window_in[:, :, row_off : row_off + lat_rows, col_off : col_off + lon_cols]
        running = running + jnp.einsum(
            "fc,bcin->bfin", conv_weight[tap_index], piece, preferred_element_type=jnp.float32
        )
    return running


def block_terms(window_in, conv_weight, kv_weight, queries, lat_rows, lon_cols):
    samples = window_in.shape[0]
    convolved = convolve_block(window_in, conv_weight, lat_rows, lon_cols)
    block_features = jax.nn.gelu(convolved, approximate=True).astype(jnp.bfloat16)
    flattened = block_features.reshape(samples, block_features.shape[1], lat_rows * lon_cols)
    key_value = jnp.einsum(
        "of,bfn->bon", kv_weight, flattened, preferred_element_type=jnp.float32
    ).astype(jnp.bfloat16)
    key_heads = key_value[:, :DL].reshape(samples, HEADS, HD, lat_rows * lon_cols)
    value_heads = key_value[:, DL:].reshape(samples, HEADS, HD, lat_rows * lon_cols)
    query_heads = queries.reshape(Q, HEADS, HD)
    scores = jnp.einsum(
        "qhd,bhdn->bhqn", query_heads, key_heads, preferred_element_type=jnp.float32
    ) * HD ** (-0.5)
    maxima = jnp.max(scores, axis=-1)
    exponent = jnp.exp(scores - maxima[..., None])
    totals = jnp.sum(exponent, axis=-1)
    weights_bf = exponent.astype(jnp.bfloat16)
    weighted = jnp.einsum(
        "bhqn,bhdn->bqhd", weights_bf, value_heads, preferred_element_type=jnp.float32
    )
    return (block_features, maxima, totals, weighted.reshape(samples, Q, DL))


def rescale(weighted, factor):
    full_shape = weighted.shape
    heads_view = weighted.reshape(full_shape[0], full_shape[1], factor.shape[1], -1)
    return (heads_view * jnp.transpose(factor, (0, 2, 1))[..., None]).reshape(full_shape)


def normalize(weighted, totals):
    full_shape = weighted.shape
    heads_view = weighted.reshape(full_shape[0], full_shape[1], totals.shape[1], -1)
    return (heads_view / jnp.transpose(totals, (0, 2, 1))[..., None]).reshape(full_shape)


def combine_partial(earlier, later):
    highest = jnp.maximum(earlier[0], later[0])
    scale_one = jnp.exp(earlier[0] - highest)
    scale_two = jnp.exp(later[0] - highest)
    totals = earlier[1] * scale_one + later[1] * scale_two
    weighted = rescale(earlier[2], scale_one) + rescale(later[2], scale_two)
    return (highest, totals, weighted)


def per_device(fields, conv_weight, kv_weight, out_weight, norm_gain, queries):
    samples, channels, lat_rows, lon_cols = fields.shape
    widened = extended(fields, (("lon", 3),), 1, True)
    padded = extended(widened, (("lat", 2),), 1, False)
    block_count = lat_rows // BLK
    initial = (
        jnp.full((samples, HEADS, Q), -1e30, jnp.float32),
        jnp.zeros((samples, HEADS, Q), jnp.float32),
        jnp.zeros((samples, Q, DL), jnp.float32),
    )

    def scan_step(running_state, block_index):
        zero_index = jnp.zeros((), jnp.int32)
        window_in = lax.dynamic_slice(
            padded,
            (zero_index, zero_index, block_index * BLK, zero_index),
            (samples, channels, BLK + 2, lon_cols + 2),
        )
        block_features, maxima, totals, weighted = block_terms(
            window_in, conv_weight, kv_weight, queries, BLK, lon_cols
        )
        return (combine_partial(running_state, (maxima, totals, weighted)), block_features)

    running_state, feats = lax.scan(scan_step, initial, jnp.arange(block_count, dtype=jnp.int32))
    features = jnp.transpose(feats, (1, 2, 0, 3, 4)).reshape(
        samples, feats.shape[2], lat_rows, lon_cols
    )
    maxima, totals, weighted = running_state
    peak = lax.pmax(maxima, ("lat", "lon"))
    factor = jnp.exp(maxima - peak)
    total_all, weighted_all = lax.psum((totals * factor, rescale(weighted, factor)), ("lat", "lon"))
    attended = normalize(weighted_all, total_all).astype(jnp.bfloat16)
    projected = jnp.einsum("bqe,ef->bqf", attended, out_weight, preferred_element_type=jnp.float32)
    latents = (
        projected
        * lax.rsqrt(jnp.mean(projected * projected, axis=-1, keepdims=True) + 1e-06)
        * norm_gain
    )
    return (features, latents)


def solution(mesh):
    in_specs = (P(None, None, "lat", "lon"), P(), P(), P(), P(), P())
    out_specs = (P(None, None, "lat", "lon"), P())
    return jax.shard_map(
        per_device, mesh=mesh, in_specs=in_specs, out_specs=out_specs, check_vma=False
    )
```

profile of v0, /device:TPU:1, one launch (start us, length us, event | category | flops | bytes accessed | tf_op | source)
XLA Modules:
  0.0 357.0 jit_solution(6077732282394592555)
XLA Ops:
  7.2 4.0 %fusion.74 = (bf16[4,69,24,1]{3,2,1,0:T(8,128)(2,1)}, bf16[4,69,24,1]{3,2,1,0:T(8,128)(2,1)S(1)}) fusion(bf16[4,69,24,128]{3,2,1,0:T(8,128)(2,1)} %param.8), kind=kLoop, calls=%fused_computation.92 | loop fusion | bytes 52992 | tf_op jit(solution)/shard_map/slice | solution.py:21
  11.2 2.2 copy.56
  13.4 2.8 collective-permute-start
  24.1 4.2 %collective-permute-start.2 = (bf16[4,69,1,130]{3,1,2,0:T(8,128)(2,1)S(1)}, bf16[4,69,1,130]{3,1,2,0:T(8,128)(2,1)}, u32[]{:S(2)}, u32[]{:S(2)}) collective-permute-start(bf16[4,69,1,130]{3,1,2,0:T(8,128)(2,1)S(1)} %get-tuple-element.150), channel_id=1, source_target_pairs={{0,32},{32,64},{64,96},{1,33},{33,65},{65,97},{2,34},{34,66},{66,9... | collective-permute-start | bytes 215288 | tf_op jit(solution)/shard_map/ppermute | solution.py:20
  29.8 4.5 %collective-permute-done.3 = bf16[4,69,1,130]{3,1,2,0:T(8,128)(2,1)} collective-permute-done((bf16[4,69,1,130]{3,1,2,0:T(8,128)(2,1)S(1)}, bf16[4,69,1,130]{3,1,2,0:T(8,128)(2,1)}, u32[]{:S(2)}, u32[]{:S(2)}) %collective-permute-start.3) | collective-permute-done | bytes 71792 | tf_op jit(solution)/shard_map/ppermute | solution.py:23
  34.3 5.1 %pad_maximum_fusion = bf16[4,69,26,130]{3,1,2,0:T(8,128)(2,1)} fusion(bf16[4,69,1,130]{3,1,2,0:T(8,128)(2,1)} %collective-permute-done.3, bf16[4,69,24,1]{3,1,2,0:T(8,128)(2,1)} %copy.32, bf16[4,69,24,128]{3,1,2,0:T(8,128)(2,1)S(1)} %copy.31, bf16[4,69,24,1]{3,1,2,0:T(8,128)(2,1)} %copy.30, bf16[4,69,1,130]{3,1,2,0:T(8,128)(2,1)} %collective-permute-done.2), kind=kLoop, calls=%fused_computation.76 | loop fusion | flops 9328800 | bytes 3731520 | tf_op jit(solution)/shard_map/concatenate | solution.py:24
  39.5 92.3 %while.17 = (s32[]{:T(128)}, f32[4,4,256]{2,0,1:T(4,128)}, f32[4,4,256]{2,0,1:T(4,128)}, f32[4,256,256]{1,2,0:T(8,128)S(1)}, bf16[3,4,128,8,128]{2,4,3,1,0:T(8,1...) while((s32[]{:T(128)}, f32[4,4,256]{2,0,1:T(4,128)}, ...), condition=%wide.region_3.4_spmd.clone, body=%wide.region_0.3_spmd.clone.sunk | while | flops 2299035648 | bytes 122200216 | solution.py:108
  42.9 2.1 fusion.136
  50.1 2.8 bitcast_dynamic-update-slice_fusion.2
  54.6 2.4 bitcast_reduce_fusion.2
  57.0 5.7 %fusion.144 = (bf16[4,4,256,1024]{2,3,0,1:T(8,128)(2,1)}, f32[4,4,256]{2,0,1:T(4,128)}) fusion(f32[4,4,1024,256]{3,2,1,0:T(8,128)S(1)} %get-tuple-element.235, f32[4,4,256]{2,0,1:T(4,128)S(1)} %get-tuple-element.233), kind=kLoop, calls=%fused_computation.3.clone.1 | loop fusion | flops 16773120 | bytes 25198592 | tf_op jit(solution)/shard_map/while/body/eval_jaxpr/convert_element_type | solution.py:57
  64.1 4.8 %fusion.146 = f32[4,256,4,64]{1,3,2,0:T(8,128)S(1)} fusion(bf16[4,4,64,1024]{3,2,1,0:T(8,128)(2,1)S(1)} %bitcast.183, bf16[4,4,256,1024]{2,3,0,1:T(8,128)(2,1)} %get-tuple-element.239, f32[4,256,4]{1,2,0:T(4,128)S(1)} %copy.74), kind=kOutput, calls=%fused_computation.20.clone.1 | convolution fusion | flops 537133056 | bytes 11550720 | tf_op jit(solution)/shard_map/while/body/eval_jaxpr/bhqn,bhdn->bqhd/dot_general | solution.py:58
  80.3 2.8 bitcast_dynamic-update-slice_fusion.2
  84.8 2.4 bitcast_reduce_fusion.2
  87.2 5.7 %fusion.144 = (bf16[4,4,256,1024]{2,3,0,1:T(8,128)(2,1)}, f32[4,4,256]{2,0,1:T(4,128)}) fusion(f32[4,4,1024,256]{3,2,1,0:T(8,128)S(1)} %get-tuple-element.235, f32[4,4,256]{2,0,1:T(4,128)S(1)} %get-tuple-element.233), kind=kLoop, calls=%fused_computation.3.clone.1 | loop fusion | flops 16773120 | bytes 25198592 | tf_op jit(solution)/shard_map/while/body/eval_jaxpr/convert_element_type | solution.py:57
  95.1 4.8 %fusion.146 = f32[4,256,4,64]{1,3,2,0:T(8,128)S(1)} fusion(bf16[4,4,64,1024]{3,2,1,0:T(8,128)(2,1)S(1)} %bitcast.183, bf16[4,4,256,1024]{2,3,0,1:T(8,128)(2,1)} %get-tuple-element.239, f32[4,256,4]{1,2,0:T(4,128)S(1)} %copy.74), kind=kOutput, calls=%fused_computation.20.clone.1 | convolution fusion | flops 537133056 | bytes 11550720 | tf_op jit(solution)/shard_map/while/body/eval_jaxpr/bhqn,bhdn->bqhd/dot_general | solution.py:58
  111.3 2.7 bitcast_dynamic-update-slice_fusion.2
  115.7 2.4 bitcast_reduce_fusion.2
  118.1 5.7 %fusion.144 = (bf16[4,4,256,1024]{2,3,0,1:T(8,128)(2,1)}, f32[4,4,256]{2,0,1:T(4,128)}) fusion(f32[4,4,1024,256]{3,2,1,0:T(8,128)S(1)} %get-tuple-element.235, f32[4,4,256]{2,0,1:T(4,128)S(1)} %get-tuple-element.233), kind=kLoop, calls=%fused_computation.3.clone.1 | loop fusion | flops 16773120 | bytes 25198592 | tf_op jit(solution)/shard_map/while/body/eval_jaxpr/convert_element_type | solution.py:57
  126.0 4.8 %fusion.146 = f32[4,256,4,64]{1,3,2,0:T(8,128)S(1)} fusion(bf16[4,4,64,1024]{3,2,1,0:T(8,128)(2,1)S(1)} %bitcast.183, bf16[4,4,256,1024]{2,3,0,1:T(8,128)(2,1)} %get-tuple-element.239, f32[4,256,4]{1,2,0:T(4,128)S(1)} %copy.74), kind=kOutput, calls=%fused_computation.20.clone.1 | convolution fusion | flops 537133056 | bytes 11550720 | tf_op jit(solution)/shard_map/while/body/eval_jaxpr/bhqn,bhdn->bqhd/dot_general | solution.py:58
  131.8 68.2 %pmax.7 = f32[4,4,256]{2,0,1:T(4,128)S(1)} all-reduce(f32[4,4,256]{2,0,1:T(4,128)} %get-tuple-element.59), channel_id=1, replica_groups=mesh['lat'=4,'lon'=32] {'lat','lon'}, use_global_device_ids=true, to_apply=%region_4.5 | all-reduce | flops 4096 | bytes 32768 | tf_op jit(solution)/shard_map/pmax | solution.py:113
  201.8 63.9 %psum.15 = f32[4,256,4]{1,0,2:T(4,128)S(1)} all-reduce(f32[4,256,4]{1,0,2:T(4,128)S(1)} %get-tuple-element.154), channel_id=1, replica_groups=mesh['lat'=4,'lon'=32] {'lat','lon'}, use_global_device_ids=true, to_apply=%region_6.7 | all-reduce | flops 4096 | bytes 32768 | tf_op jit(solution)/shard_map/psum | solution.py:115
  265.8 4.8 %copy.34 = bf16[4,128,3,8,128]{4,3,2,1,0:T(8,128)(2,1)} copy(bf16[4,128,3,8,128]{1,4,3,0,2:T(8,128)(2,1)} %bitcast.185) | data formatting | bytes 6291456 | tf_op jit(solution)/shard_map/transpose | solution.py:109
  270.6 76.4 %all-reduce.2.cloned.1.call-done = f32[4,256,256]{1,2,0:T(8,128)} async-done(((f32[4,256,256]{1,2,0:T(8,128)}), f32[4,256,256]{1,2,0:T(8,128)}) %all-reduce.2.cloned.1.call-update) | async-done | bytes 1048592 | tf_op jit(solution)/shard_map/psum | solution.py:115
  (109 shorter events, 54.9 us)
Async XLA Ops:
  7.2 341.1 %copy-start = (bf16[256,256]{1,0:T(8,128)(2,1)S(1)}, bf16[256,256]{1,0:T(8,128)(2,1)}, u32[]{:S(2)}) copy-start(bf16[256,256]{1,0:T(8,128)(2,1)} %param.11) | copy-start | bytes 393220
  7.2 339.8 %all-reduce.2.cloned.1.call-start = ((), (), s32[]{:S(2)}) async-start(), calls=%async_computation | async-start | bytes 2097152 | tf_op jit(solution)/shard_map/psum | solution.py:115
  13.4 5.7 %collective-permute-start = (bf16[4,69,24,1]{1,2,3,0:T(8,128)(2,1)S(1)}, bf16[4,69,24,1]{1,2,3,0:T(8,128)(2,1)S(1)}, u32[]{:S(2)}, u32[]{:S(2)}) collective-permute-start(bf16[4,69,24,1]{1,2,3,0:T(8,128)(2,1)S(1)} %copy.56), channel_id=1, source_target_pairs={{0,1},{1,2},{2,3},{3,4},{4,5},{5,6},{6,7},{7,8},{8,9},{9,10},{10,1... | collective-permute-start | bytes 39752 | tf_op jit(solution)/shard_map/ppermute | solution.py:20
  17.3 3.7 %collective-permute-start.1 = (bf16[4,69,24,1]{1,2,3,0:T(8,128)(2,1)S(1)}, bf16[4,69,24,1]{1,2,3,0:T(8,128)(2,1)S(1)}, u32[]{:S(2)}, u32[]{:S(2)}) collective-permute-start(bf16[4,69,24,1]{1,2,3,0:T(8,128)(2,1)S(1)} %copy.57), channel_id=1, source_target_pairs={{1,0},{2,1},{3,2},{4,3},{5,4},{6,5},{7,6},{8,7},{9,8},{10,9},{11,1... | collective-permute-start | bytes 39752 | tf_op jit(solution)/shard_map/ppermute | solution.py:23
  22.9 6.8 %copy-start.4 = (bf16[256,256]{1,0:T(8,128)(2,1)S(1)}, bf16[256,256]{1,0:T(8,128)(2,1)}, u32[]{:S(2)}) copy-start(bf16[256,256]{1,0:T(8,128)(2,1)} %param.13) | copy-start | bytes 393220
  24.1 5.7 %collective-permute-start.2 = (bf16[4,69,1,130]{3,1,2,0:T(8,128)(2,1)S(1)}, bf16[4,69,1,130]{3,1,2,0:T(8,128)(2,1)}, u32[]{:S(2)}, u32[]{:S(2)}) collective-permute-start(bf16[4,69,1,130]{3,1,2,0:T(8,128)(2,1)S(1)} %get-tuple-element.150), channel_id=1, source_target_pairs={{0,32},{32,64},{64,96},{1,33},{33,65},{65,97},{2,34},{34,66},{66,9... | collective-permute-start | bytes 215288 | tf_op jit(solution)/shard_map/ppermute | solution.py:20
  28.3 6.0 %collective-permute-start.3 = (bf16[4,69,1,130]{3,1,2,0:T(8,128)(2,1)S(1)}, bf16[4,69,1,130]{3,1,2,0:T(8,128)(2,1)}, u32[]{:S(2)}, u32[]{:S(2)}) collective-permute-start(bf16[4,69,1,130]{3,1,2,0:T(8,128)(2,1)S(1)} %get-tuple-element.151), channel_id=1, source_target_pairs={{32,0},{64,32},{96,64},{33,1},{65,33},{97,65},{34,2},{66,34},{98,6... | collective-permute-start | bytes 215288 | tf_op jit(solution)/shard_map/ppermute | solution.py:23
  29.8 9.7 %copy-start.3 = (bf16[512,128]{1,0:T(8,128)(2,1)S(1)}, bf16[512,128]{1,0:T(8,128)(2,1)}, u32[]{:S(2)}) copy-start(bf16[512,128]{1,0:T(8,128)(2,1)} %param.10) | copy-start | bytes 393220
  39.6 1.3 copy-start.6
  42.9 4.2 %copy-start.1 = (bf16[4,69,26,130]{3,1,2,0:T(8,128)(2,1)S(1)}, bf16[4,69,26,130]{3,1,2,0:T(8,128)(2,1)}, u32[]{:S(2)}) copy-start(bf16[4,69,26,130]{3,1,2,0:T(8,128)(2,1)} %get-tuple-element.281) | copy-start | bytes 5597284 | tf_op jit(solution)/shard_map/while
  42.9 4.2 %copy-start.2 = (bf16[9,128,69]{1,2,0:T(8,128)(2,1)S(1)}, bf16[9,128,69]{1,2,0:T(8,128)(2,1)}, u32[]{:S(2)}) copy-start(bf16[9,128,69]{1,2,0:T(8,128)(2,1)} %get-tuple-element.282) | copy-start | bytes 476932 | tf_op jit(solution)/shard_map/while
  68.9 1.0 copy-start.7
  69.9 1.2 copy-start.6
  73.2 4.2 %copy-start.1 = (bf16[4,69,26,130]{3,1,2,0:T(8,128)(2,1)S(1)}, bf16[4,69,26,130]{3,1,2,0:T(8,128)(2,1)}, u32[]{:S(2)}) copy-start(bf16[4,69,26,130]{3,1,2,0:T(8,128)(2,1)} %get-tuple-element.281) | copy-start | bytes 5597284 | tf_op jit(solution)/shard_map/while
  73.2 4.2 %copy-start.2 = (bf16[9,128,69]{1,2,0:T(8,128)(2,1)S(1)}, bf16[9,128,69]{1,2,0:T(8,128)(2,1)}, u32[]{:S(2)}) copy-start(bf16[9,128,69]{1,2,0:T(8,128)(2,1)} %get-tuple-element.282) | copy-start | bytes 476932 | tf_op jit(solution)/shard_map/while
  99.9 1.0 copy-start.7
  100.8 1.2 copy-start.6
  104.1 4.2 %copy-start.1 = (bf16[4,69,26,130]{3,1,2,0:T(8,128)(2,1)S(1)}, bf16[4,69,26,130]{3,1,2,0:T(8,128)(2,1)}, u32[]{:S(2)}) copy-start(bf16[4,69,26,130]{3,1,2,0:T(8,128)(2,1)} %get-tuple-element.281) | copy-start | bytes 5597284 | tf_op jit(solution)/shard_map/while
  104.1 4.2 %copy-start.2 = (bf16[9,128,69]{1,2,0:T(8,128)(2,1)S(1)}, bf16[9,128,69]{1,2,0:T(8,128)(2,1)}, u32[]{:S(2)}) copy-start(bf16[9,128,69]{1,2,0:T(8,128)(2,1)} %get-tuple-element.282) | copy-start | bytes 476932 | tf_op jit(solution)/shard_map/while
  130.8 1.0 copy-start.7
  270.6 78.1 %copy-start.5 = (f32[256]{0:T(256)S(1)}, f32[256]{0:T(256)}, u32[]{:S(2)}) copy-start(f32[256]{0:T(256)} %param.12) | copy-start | bytes 3076
Sparse Core Ops, SparseCore 0:
  201.9 144.9 all-reduce.1
where the time goes:
time: 358 us; the launch traced here: 357 us
  blocking collectives  132 us (37%)
  waiting for transfers between devices  80.9 us (23%)
  matrix products  61.3 us (17%)
  other arithmetic  33.4 us (9%)
  local copies, waits for them, and re-layouts  24.1 us (7%)
  between operations  14.2 us (4%)
  starting transfers between devices  8.37 us (2%)
    psum x1, waiting for transfers between devices, per_device(): lax.psum((totals * factor, rescale(weighted, factor)), ('lat', 'lon'))  76.4 us
    pmax x1, blocking collectives, per_device(): peak = lax.pmax(maxima, ('lat', 'lon'))  68.2 us
    psum x1, blocking collectives, per_device(): lax.psum((totals * factor, rescale(weighted, factor)), ('lat', 'lon'))  63.9 us
    dot_general x27, matrix products, convolve_block(): jnp.einsum('fc,bcin->bfin', conv_weight[tap_index], piece, preferred_elem...  35.6 us
    convert_element_type x3, other arithmetic, block_terms(): weights_bf = exponent.astype(jnp.bfloat16)  17.2 us
    dot_general x3, matrix products, block_terms(): jnp.einsum('bhqn,bhdn->bqhd', weights_bf, value_heads, preferred_element_...  14.4 us
    dot_general x3, matrix products, block_terms(): jnp.einsum('qhd,bhdn->bhqn', query_heads, key_heads, preferred_element_ty...  7.22 us
  transfers between devices with their start and end apart: 5, of which 2 were waited for; matrix products, arithmetic and copies ran while one was open for 3% of the time, Pallas kernels for 0%

commit v1 on v0

--- a/solution.py
+++ b/solution.py
@@ -112,7 +112,15 @@
     maxima, totals, weighted = running_state
     peak = lax.pmax(maxima, ("lat", "lon"))
     factor = jnp.exp(maxima - peak)
-    total_all, weighted_all = lax.psum((totals * factor, rescale(weighted, factor)), ("lat", "lon"))
+
+    def order_limits(content, net_axis, a_name):
+        f_next = lax.psum(content, net_axis)
+        last = lax.psum(f_next, a_name)
+        return last
+
+    total_all, weighted_all = order_limits(
+        (totals * factor, rescale(weighted, factor)), "lat", "lon"
+    )
     attended = normalize(weighted_all, total_all).astype(jnp.bfloat16)
     projected = jnp.einsum("bqe,ef->bqf", attended, out_weight, preferred_element_type=jnp.float32)
     latents = (

time: 358 us -> 401 us (1.12); the launches traced: 357 us -> 395 us
  blocking collectives: 132 us -> 205 us
  waiting for transfers between devices: 80.9 us -> 46.7 us
    psum x1 -> x2, blocking collectives: 63.9 us -> 136 us  [the longest x1 124 us: order_limits(): last = lax.psum(f_next, a_name)]
    psum x1 -> x2, waiting for transfers between devices: 76.4 us -> 42.2 us  [the longest x1 42.2 us: order_limits(): f_next = lax.psum(content, net_axis)]
  transfers between devices with their start and end apart: 5 -> 6, of which waited for: 2 -> 2; matrix products, arithmetic and copies ran while one was open for 3% -> 2% of each run, Pallas kernels for 0% -> 0%
where the time goes in v1:
time: 401 us; the launch traced here: 395 us
  blocking collectives  205 us (51%)
  matrix products  61.3 us (15%)
  waiting for transfers between devices  46.7 us (12%)
  other arithmetic  33.4 us (8%)
  local copies, waits for them, and re-layouts  24.1 us (6%)
  between operations  14.2 us (4%)
  starting transfers between devices  8.39 us (2%)
    psum x1, blocking collectives, order_limits(): last = lax.psum(f_next, a_name)  124 us
    pmax x1, blocking collectives, per_device(): peak = lax.pmax(maxima, ('lat', 'lon'))  68.2 us
    psum x1, waiting for transfers between devices, order_limits(): f_next = lax.psum(content, net_axis)  42.2 us
    dot_general x27, matrix products, convolve_block(): jnp.einsum('fc,bcin->bfin', conv_weight[tap_index], piece, preferred_elem...  35.6 us
    convert_element_type x3, other arithmetic, block_terms(): weights_bf = exponent.astype(jnp.bfloat16)  17.1 us
    dot_general x3, matrix products, block_terms(): jnp.einsum('bhqn,bhdn->bqhd', weights_bf, value_heads, preferred_element_...  14.4 us
    psum x1, blocking collectives, order_limits(): f_next = lax.psum(content, net_axis)  12.7 us
  transfers between devices with their start and end apart: 6, of which 2 were waited for; matrix products, arithmetic and copies ran while one was open for 2% of the time, Pallas kernels for 0%

profile of v1, /device:TPU:1, one launch (start us, length us, event | category | flops | bytes accessed | tf_op | source)
XLA Modules:
  0.0 395.2 jit_solution(5847579589919727448)
XLA Ops:
  7.2 4.0 %fusion.75 = (bf16[4,69,24,1]{3,2,1,0:T(8,128)(2,1)}, bf16[4,69,24,1]{3,2,1,0:T(8,128)(2,1)S(1)}) fusion(bf16[4,69,24,128]{3,2,1,0:T(8,128)(2,1)} %param.8), kind=kLoop, calls=%fused_computation.92 | loop fusion | bytes 52992 | tf_op jit(solution)/shard_map/slice | solution.py:21
  11.2 2.2 copy.56
  13.4 2.8 collective-permute-start
  24.1 4.2 %collective-permute-start.2 = (bf16[4,69,1,130]{3,1,2,0:T(8,128)(2,1)S(1)}, bf16[4,69,1,130]{3,1,2,0:T(8,128)(2,1)}, u32[]{:S(2)}, u32[]{:S(2)}) collective-permute-start(bf16[4,69,1,130]{3,1,2,0:T(8,128)(2,1)S(1)} %get-tuple-element.150), channel_id=1, source_target_pairs={{0,32},{32,64},{64,96},{1,33},{33,65},{65,97},{2,34},{34,66},{66,9... | collective-permute-start | bytes 215288 | tf_op jit(solution)/shard_map/ppermute | solution.py:20
  29.8 4.5 %collective-permute-done.3 = bf16[4,69,1,130]{3,1,2,0:T(8,128)(2,1)} collective-permute-done((bf16[4,69,1,130]{3,1,2,0:T(8,128)(2,1)S(1)}, bf16[4,69,1,130]{3,1,2,0:T(8,128)(2,1)}, u32[]{:S(2)}, u32[]{:S(2)}) %collective-permute-start.3) | collective-permute-done | bytes 71792 | tf_op jit(solution)/shard_map/ppermute | solution.py:23
  34.3 5.1 %pad_maximum_fusion = bf16[4,69,26,130]{3,1,2,0:T(8,128)(2,1)} fusion(bf16[4,69,1,130]{3,1,2,0:T(8,128)(2,1)} %collective-permute-done.3, bf16[4,69,24,1]{3,1,2,0:T(8,128)(2,1)} %copy.32, bf16[4,69,24,128]{3,1,2,0:T(8,128)(2,1)S(1)} %copy.31, bf16[4,69,24,1]{3,1,2,0:T(8,128)(2,1)} %copy.30, bf16[4,69,1,130]{3,1,2,0:T(8,128)(2,1)} %collective-permute-done.2), kind=kLoop, calls=%fused_computation.76 | loop fusion | flops 9328800 | bytes 3731520 | tf_op jit(solution)/shard_map/concatenate | solution.py:24
  39.4 92.2 %while.17 = (s32[]{:T(128)}, f32[4,4,256]{2,0,1:T(4,128)}, f32[4,4,256]{2,0,1:T(4,128)}, f32[4,256,256]{1,2,0:T(8,128)S(1)}, bf16[3,4,128,8,128]{2,4,3,1,0:T(8,1...) while((s32[]{:T(128)}, f32[4,4,256]{2,0,1:T(4,128)}, ...), condition=%wide.region_3.4_spmd.clone, body=%wide.region_0.3_spmd.clone.sunk | while | flops 2299035648 | bytes 122200216 | solution.py:108
  50.1 2.8 bitcast_dynamic-update-slice_fusion.2
  54.6 2.4 bitcast_reduce_fusion.2
  57.0 5.7 %fusion.145 = (bf16[4,4,256,1024]{2,3,0,1:T(8,128)(2,1)}, f32[4,4,256]{2,0,1:T(4,128)}) fusion(f32[4,4,1024,256]{3,2,1,0:T(8,128)S(1)} %get-tuple-element.235, f32[4,4,256]{2,0,1:T(4,128)S(1)} %get-tuple-element.233), kind=kLoop, calls=%fused_computation.3.clone.1 | loop fusion | flops 16773120 | bytes 25198592 | tf_op jit(solution)/shard_map/while/body/eval_jaxpr/convert_element_type | solution.py:57
  64.1 4.8 %fusion.147 = f32[4,256,4,64]{1,3,2,0:T(8,128)S(1)} fusion(bf16[4,4,64,1024]{3,2,1,0:T(8,128)(2,1)S(1)} %bitcast.182, bf16[4,4,256,1024]{2,3,0,1:T(8,128)(2,1)} %get-tuple-element.239, f32[4,256,4]{1,2,0:T(4,128)S(1)} %copy.74), kind=kOutput, calls=%fused_computation.20.clone.1 | convolution fusion | flops 537133056 | bytes 11550720 | tf_op jit(solution)/shard_map/while/body/eval_jaxpr/bhqn,bhdn->bqhd/dot_general | solution.py:58
  80.3 2.8 bitcast_dynamic-update-slice_fusion.2
  84.7 2.4 bitcast_reduce_fusion.2
  87.2 5.7 %fusion.145 = (bf16[4,4,256,1024]{2,3,0,1:T(8,128)(2,1)}, f32[4,4,256]{2,0,1:T(4,128)}) fusion(f32[4,4,1024,256]{3,2,1,0:T(8,128)S(1)} %get-tuple-element.235, f32[4,4,256]{2,0,1:T(4,128)S(1)} %get-tuple-element.233), kind=kLoop, calls=%fused_computation.3.clone.1 | loop fusion | flops 16773120 | bytes 25198592 | tf_op jit(solution)/shard_map/while/body/eval_jaxpr/convert_element_type | solution.py:57
  95.0 4.8 %fusion.147 = f32[4,256,4,64]{1,3,2,0:T(8,128)S(1)} fusion(bf16[4,4,64,1024]{3,2,1,0:T(8,128)(2,1)S(1)} %bitcast.182, bf16[4,4,256,1024]{2,3,0,1:T(8,128)(2,1)} %get-tuple-element.239, f32[4,256,4]{1,2,0:T(4,128)S(1)} %copy.74), kind=kOutput, calls=%fused_computation.20.clone.1 | convolution fusion | flops 537133056 | bytes 11550720 | tf_op jit(solution)/shard_map/while/body/eval_jaxpr/bhqn,bhdn->bqhd/dot_general | solution.py:58
  111.2 2.7 bitcast_dynamic-update-slice_fusion.2
  115.6 2.4 bitcast_reduce_fusion.2
  118.1 5.7 %fusion.145 = (bf16[4,4,256,1024]{2,3,0,1:T(8,128)(2,1)}, f32[4,4,256]{2,0,1:T(4,128)}) fusion(f32[4,4,1024,256]{3,2,1,0:T(8,128)S(1)} %get-tuple-element.235, f32[4,4,256]{2,0,1:T(4,128)S(1)} %get-tuple-element.233), kind=kLoop, calls=%fused_computation.3.clone.1 | loop fusion | flops 16773120 | bytes 25198592 | tf_op jit(solution)/shard_map/while/body/eval_jaxpr/convert_element_type | solution.py:57
  125.9 4.8 %fusion.147 = f32[4,256,4,64]{1,3,2,0:T(8,128)S(1)} fusion(bf16[4,4,64,1024]{3,2,1,0:T(8,128)(2,1)S(1)} %bitcast.182, bf16[4,4,256,1024]{2,3,0,1:T(8,128)(2,1)} %get-tuple-element.239, f32[4,256,4]{1,2,0:T(4,128)S(1)} %copy.74), kind=kOutput, calls=%fused_computation.20.clone.1 | convolution fusion | flops 537133056 | bytes 11550720 | tf_op jit(solution)/shard_map/while/body/eval_jaxpr/bhqn,bhdn->bqhd/dot_general | solution.py:58
  131.7 68.2 %pmax.7 = f32[4,4,256]{2,0,1:T(4,128)S(1)} all-reduce(f32[4,4,256]{2,0,1:T(4,128)} %get-tuple-element.59), channel_id=1, replica_groups=mesh['lat'=4,'lon'=32] {'lat','lon'}, use_global_device_ids=true, to_apply=%region_4.5 | all-reduce | flops 4096 | bytes 32768 | tf_op jit(solution)/shard_map/pmax | solution.py:113
  201.8 42.2 %all-reduce.3.cloned.1.call-done = f32[4,256,256]{1,2,0:T(8,128)} async-done(((f32[4,256,256]{1,2,0:T(8,128)}), f32[4,256,256]{1,2,0:T(8,128)}) %all-reduce.3.cloned.1.call-update) | async-done | bytes 1048592 | tf_op jit(solution)/shard_map/psum | solution.py:117
  244.0 12.7 %psum.30 = f32[4,4,256]{2,0,1:T(4,128)S(1)} all-reduce(f32[4,4,256]{2,0,1:T(4,128)S(1)} %get-tuple-element.154), channel_id=1, replica_groups=mesh['lat'=4,'lon'=32] {'lat'}, use_global_device_ids=true, to_apply=%region_7.8 | all-reduce | flops 4096 | bytes 32768 | tf_op jit(solution)/shard_map/psum | solution.py:117
  256.7 123.7 %psum.31 = f32[4,256,4]{1,0,2:T(4,128)S(1)} all-reduce(f32[4,256,4]{1,0,2:T(4,128)S(1)} %bitcast.186), channel_id=1, replica_groups=mesh['lat'=4,'lon'=32] {'lon'}, use_global_device_ids=true, to_apply=%region_8.9 | all-reduce | flops 4096 | bytes 32768 | tf_op jit(solution)/shard_map/psum | solution.py:118
  380.4 4.8 %copy.34 = bf16[4,128,3,8,128]{4,3,2,1,0:T(8,128)(2,1)} copy(bf16[4,128,3,8,128]{1,4,3,0,2:T(8,128)(2,1)} %bitcast.184) | data formatting | bytes 6291456 | tf_op jit(solution)/shard_map/transpose | solution.py:109
  (113 shorter events, 57.1 us)
Async XLA Ops:
  7.2 379.4 %copy-start = (bf16[256,256]{1,0:T(8,128)(2,1)S(1)}, bf16[256,256]{1,0:T(8,128)(2,1)}, u32[]{:S(2)}) copy-start(bf16[256,256]{1,0:T(8,128)(2,1)} %param.11) | copy-start | bytes 393220
  7.2 236.8 %all-reduce.3.cloned.1.call-start = ((), (), s32[]{:S(2)}) async-start(), calls=%async_computation | async-start | bytes 2097152 | tf_op jit(solution)/shard_map/psum | solution.py:117
  13.4 5.7 %collective-permute-start = (bf16[4,69,24,1]{1,2,3,0:T(8,128)(2,1)S(1)}, bf16[4,69,24,1]{1,2,3,0:T(8,128)(2,1)S(1)}, u32[]{:S(2)}, u32[]{:S(2)}) collective-permute-start(bf16[4,69,24,1]{1,2,3,0:T(8,128)(2,1)S(1)} %copy.56), channel_id=1, source_target_pairs={{0,1},{1,2},{2,3},{3,4},{4,5},{5,6},{6,7},{7,8},{8,9},{9,10},{10,1... | collective-permute-start | bytes 39752 | tf_op jit(solution)/shard_map/ppermute | solution.py:20
  17.3 3.7 collective-permute-start.1
  22.9 6.8 %copy-start.4 = (bf16[256,256]{1,0:T(8,128)(2,1)S(1)}, bf16[256,256]{1,0:T(8,128)(2,1)}, u32[]{:S(2)}) copy-start(bf16[256,256]{1,0:T(8,128)(2,1)} %param.13) | copy-start | bytes 393220
  24.1 5.7 %collective-permute-start.2 = (bf16[4,69,1,130]{3,1,2,0:T(8,128)(2,1)S(1)}, bf16[4,69,1,130]{3,1,2,0:T(8,128)(2,1)}, u32[]{:S(2)}, u32[]{:S(2)}) collective-permute-start(bf16[4,69,1,130]{3,1,2,0:T(8,128)(2,1)S(1)} %get-tuple-element.150), channel_id=1, source_target_pairs={{0,32},{32,64},{64,96},{1,33},{33,65},{65,97},{2,34},{34,66},{66,9... | collective-permute-start | bytes 215288 | tf_op jit(solution)/shard_map/ppermute | solution.py:20
  28.3 6.0 %collective-permute-start.3 = (bf16[4,69,1,130]{3,1,2,0:T(8,128)(2,1)S(1)}, bf16[4,69,1,130]{3,1,2,0:T(8,128)(2,1)}, u32[]{:S(2)}, u32[]{:S(2)}) collective-permute-start(bf16[4,69,1,130]{3,1,2,0:T(8,128)(2,1)S(1)} %get-tuple-element.151), channel_id=1, source_target_pairs={{32,0},{64,32},{96,64},{33,1},{65,33},{97,65},{34,2},{66,34},{98,6... | collective-permute-start | bytes 215288 | tf_op jit(solution)/shard_map/ppermute | solution.py:23
  29.8 9.7 %copy-start.3 = (bf16[512,128]{1,0:T(8,128)(2,1)S(1)}, bf16[512,128]{1,0:T(8,128)(2,1)}, u32[]{:S(2)}) copy-start(bf16[512,128]{1,0:T(8,128)(2,1)} %param.10) | copy-start | bytes 393220
  39.6 1.3 copy-start.6
  42.9 4.2 %copy-start.1 = (bf16[4,69,26,130]{3,1,2,0:T(8,128)(2,1)S(1)}, bf16[4,69,26,130]{3,1,2,0:T(8,128)(2,1)}, u32[]{:S(2)}) copy-start(bf16[4,69,26,130]{3,1,2,0:T(8,128)(2,1)} %get-tuple-element.281) | copy-start | bytes 5597284 | tf_op jit(solution)/shard_map/while
  42.9 4.2 %copy-start.2 = (bf16[9,128,69]{1,2,0:T(8,128)(2,1)S(1)}, bf16[9,128,69]{1,2,0:T(8,128)(2,1)}, u32[]{:S(2)}) copy-start(bf16[9,128,69]{1,2,0:T(8,128)(2,1)} %get-tuple-element.282) | copy-start | bytes 476932 | tf_op jit(solution)/shard_map/while
  68.9 1.0 copy-start.7
  69.9 1.2 copy-start.6
  73.1 4.2 %copy-start.1 = (bf16[4,69,26,130]{3,1,2,0:T(8,128)(2,1)S(1)}, bf16[4,69,26,130]{3,1,2,0:T(8,128)(2,1)}, u32[]{:S(2)}) copy-start(bf16[4,69,26,130]{3,1,2,0:T(8,128)(2,1)} %get-tuple-element.281) | copy-start | bytes 5597284 | tf_op jit(solution)/shard_map/while
  73.1 4.2 %copy-start.2 = (bf16[9,128,69]{1,2,0:T(8,128)(2,1)S(1)}, bf16[9,128,69]{1,2,0:T(8,128)(2,1)}, u32[]{:S(2)}) copy-start(bf16[9,128,69]{1,2,0:T(8,128)(2,1)} %get-tuple-element.282) | copy-start | bytes 476932 | tf_op jit(solution)/shard_map/while
  99.8 1.0 copy-start.7
  100.8 1.2 copy-start.6
  104.0 4.2 %copy-start.1 = (bf16[4,69,26,130]{3,1,2,0:T(8,128)(2,1)S(1)}, bf16[4,69,26,130]{3,1,2,0:T(8,128)(2,1)}, u32[]{:S(2)}) copy-start(bf16[4,69,26,130]{3,1,2,0:T(8,128)(2,1)} %get-tuple-element.281) | copy-start | bytes 5597284 | tf_op jit(solution)/shard_map/while
  104.0 4.2 %copy-start.2 = (bf16[9,128,69]{1,2,0:T(8,128)(2,1)S(1)}, bf16[9,128,69]{1,2,0:T(8,128)(2,1)}, u32[]{:S(2)}) copy-start(bf16[9,128,69]{1,2,0:T(8,128)(2,1)} %get-tuple-element.282) | copy-start | bytes 476932 | tf_op jit(solution)/shard_map/while
  130.7 1.0 copy-start.7
  201.7 183.5 %all-reduce.5.cloned.1.call-start = ((), (), s32[]{:S(2)}) async-start(), calls=%async_computation.1 | async-start | bytes 2097152 | tf_op jit(solution)/shard_map/psum | solution.py:118
  385.2 1.7 copy-start.5
Sparse Core Ops, SparseCore 0:
  201.8 42.0 all-reduce.2
  247.5 106.7 all-reduce.4
